TPU v7x, 32 devices: a whole 2x2x4 slice. The times are simulated.
32 devices in a mesh: dom: 2 (over x), term: 16 (over z, y, core).
Axes of the slice: x: 2, y: 2, z: 4, core: 2. Of those that a mesh axis runs over, the one named last changes fastest.
Arguments:
- tile_values: bfloat16 [3072, 128, 128], P(('dom', 'term')), parts along dimension 0, may hold values from -6 to 6
- tile_doc: int32 [3072], P(('dom', 'term')), parts along dimension 0, may hold values from 0 to 31, as said below
- tile_col: int32 [3072], P(('dom', 'term')), parts along dimension 0, may hold values from 0 to 31
- tile_count: int32 [32], P('dom'), parts along dimension 0, may hold values from 1 to 96, as said below
- panel: bfloat16 [65536, 256], P('term'), may hold values from -6 to 6
Outputs:
- panel_next: float32 [131072, 256], P(('dom', 'term')), parts along dimension 0
There are 2 independent parts, one for each index of `dom`. A program takes and returns all parts, laid end to end along the dimension named above; an argument that names none is the same for every part. Nothing has to cross between parts.
Inputs may be any that keep to these rules, and one draw needn't show every extreme that they name: Within one device's 96 slots the pairs (tile_doc, tile_col) are all different. Slots of device d at or above tile_count[d] are not part of the matrix; terms are in order of falling frequency, so tile_count[d] lies between 96 - 77 * d // 15 - 12 and 96 - 77 * d // 15, and tile_count[0] is 96.
All inputs are finite; a program needn't handle non-finite values.
Results may differ from a plain program's by a relative error of at most 0.0095.
Values may be sent and summed in bfloat16 or wider, within the bound.
A program may use at most 64 MiB of HBM per device.

v0:
```python
import jax
import jax.numpy as jnp
from jax import lax
from jax.sharding import PartitionSpec as P

DOC_BLKS = 32


shift_ratio = 0.001
block_slots = 8


def factor(gram_matrix):
    rank_width = gram_matrix.shape[0]
    shifted = gram_matrix + shift_ratio * jnp.trace(gram_matrix) / rank_width * jnp.eye(
        rank_width, dtype=jnp.float32
    )
    return jnp.linalg.cholesky(shifted)


def whiten(chol_lower, row_block):
    return jax.scipy.linalg.solve_triangular(chol_lower, row_block.T, lower=True).T


def local(tile_values, tile_doc, tile_col, tile_count, panel):
    tile_size = tile_values.shape[1]
    rank_width = panel.shape[1]
    term_blocks = panel.shape[0] // tile_size
    doc_blocks = DOC_BLKS
    q_blocks = panel.reshape(term_blocks, tile_size, rank_width)
    own_index = lax.axis_index("term")
    own_count = tile_count[own_index]
    slot_ids = jnp.arange(block_slots, dtype=jnp.int32)
    doc_ids = jnp.arange(doc_blocks, dtype=jnp.int32)
    col_ids = jnp.arange(term_blocks, dtype=jnp.int32)

    def slot_block(offset, end_slot):
        tiles_now = lax.dynamic_slice_in_dim(tile_values, offset, block_slots, 0)
        docs_now = lax.dynamic_slice_in_dim(tile_doc, offset, block_slots, 0)
        cols_now = lax.dynamic_slice_in_dim(tile_col, offset, block_slots, 0)
        live_mask = (offset + slot_ids < end_slot).astype(jnp.float32)
        return (tiles_now, docs_now, cols_now, live_mask)

    def forward(summed, tiles_now, picked, one_hot):
        products = jnp.einsum("sij,sjr->sir", tiles_now, picked, preferred_element_type=jnp.float32)
        return summed + jnp.einsum("sd,sir->dir", one_hot, products)

    def backward(summed, tiles_now, picked, one_hot):
        products = jnp.einsum("sij,sir->sjr", tiles_now, picked, preferred_element_type=jnp.float32)
        return summed + jnp.einsum("sc,sjr->cjr", one_hot, products)

    doc_sums = jnp.zeros((doc_blocks, tile_size, rank_width), jnp.float32)

    def step_fwd(step_index, carried):
        tiles_now, docs_now, cols_now, live_mask = slot_block(step_index * block_slots, own_count)
        one_hot = (docs_now[:, None] == doc_ids[None, :]).astype(jnp.float32) * live_mask[:, None]
        return forward(carried, tiles_now, jnp.take(q_blocks, cols_now, axis=0), one_hot)

    doc_sums = lax.fori_loop(0, (own_count + block_slots - 1) // block_slots, step_fwd, doc_sums)
    row_sums = doc_sums.reshape(doc_blocks * tile_size, rank_width)
    whole_rows = lax.psum(row_sums, "term")
    gram_matrix = jnp.dot(whole_rows.T, whole_rows, precision=lax.Precision.HIGHEST)
    ortho_rows = whiten(factor(gram_matrix), whole_rows).astype(jnp.bfloat16)
    ortho_blocks = ortho_rows.reshape(doc_blocks, tile_size, rank_width)
    panel_sums = jnp.zeros((term_blocks, tile_size, rank_width), jnp.float32)

    def step_bwd(step_index, carried):
        tiles_now, docs_now, cols_now, live_mask = slot_block(step_index * block_slots, own_count)
        one_hot = (cols_now[:, None] == col_ids[None, :]).astype(jnp.float32) * live_mask[:, None]
        return backward(carried, tiles_now, jnp.take(ortho_blocks, docs_now, axis=0), one_hot)

    panel_sums = lax.fori_loop(
        0, (own_count + block_slots - 1) // block_slots, step_bwd, panel_sums
    )
    return panel_sums.reshape(term_blocks * tile_size, rank_width)


def solution(mesh):
    return jax.shard_map(
        local,
        mesh=mesh,
        in_specs=(
            P(("dom", "term"), None, None),
            P(("dom", "term")),
            P(("dom", "term")),
            P("dom"),
            P("term", None),
        ),
        out_specs=P(("dom", "term"), None),
        check_vma=False,
    )
```

profile of v0, /device:TPU:0, one launch (start us, length us, event | category | flops | bytes accessed | tf_op | source)
XLA Modules:
  0.0 434.5 jit_solution(16957462485810426433)
XLA Ops:
  11.0 112.8 %while.24 = (s32[]{:T(128)}, f32[32,128,256]{2,0,1:T(8,128)}, s32[]{:T(128)}, s32[96]{0:T(128)S(1)}, s32[]{:T(128)}, /*index=5*/bf16[96,128,128]{2,1,0:T(8,128)(...) while((s32[]{:T(128)}, f32[32,128,256]{2,0,1:T(8,128)}, ...), condition=%wide.region_1.3_spmd.clone, body=%wide.region_0.2_spmd.clone.sunk | while | flops 85198416 | bytes 11276743 | solution.py:59
  15.3 5.1 %convolution_add_fusion.4 = f32[32,128,256]{2,0,1:T(8,128)} fusion(f32[32,128,256]{2,0,1:T(8,128)} %get-tuple-element.392, bf16[8,128,256]{2,1,0:T(8,128)(2,1)S(1)} %fusion.68, bf16[8]{0:T(256)(128)(2,1)S(1)} %get-tuple-element.367, s32[8]{0:T(128)S(1)} %dynamic_slice.41), kind=kOutput, calls=%fused_computation.8.clone.1 | convolution fusion | flops 17826304 | bytes 8912944 | tf_op jit(solution)/shard_map/while/body/sd,sir->dir/dot_general | solution.py:46
  24.7 5.1 %convolution_add_fusion.4 = f32[32,128,256]{2,0,1:T(8,128)} fusion(f32[32,128,256]{2,0,1:T(8,128)} %get-tuple-element.392, bf16[8,128,256]{2,1,0:T(8,128)(2,1)S(1)} %fusion.68, bf16[8]{0:T(256)(128)(2,1)S(1)} %get-tuple-element.367, s32[8]{0:T(128)S(1)} %dynamic_slice.41), kind=kOutput, calls=%fused_computation.8.clone.1 | convolution fusion | flops 17826304 | bytes 8912944 | tf_op jit(solution)/shard_map/while/body/sd,sir->dir/dot_general | solution.py:46
  34.1 5.1 %convolution_add_fusion.4 = f32[32,128,256]{2,0,1:T(8,128)} fusion(f32[32,128,256]{2,0,1:T(8,128)} %get-tuple-element.392, bf16[8,128,256]{2,1,0:T(8,128)(2,1)S(1)} %fusion.68, bf16[8]{0:T(256)(128)(2,1)S(1)} %get-tuple-element.367, s32[8]{0:T(128)S(1)} %dynamic_slice.41), kind=kOutput, calls=%fused_computation.8.clone.1 | convolution fusion | flops 17826304 | bytes 8912944 | tf_op jit(solution)/shard_map/while/body/sd,sir->dir/dot_general | solution.py:46
  43.5 5.1 %convolution_add_fusion.4 = f32[32,128,256]{2,0,1:T(8,128)} fusion(f32[32,128,256]{2,0,1:T(8,128)} %get-tuple-element.392, bf16[8,128,256]{2,1,0:T(8,128)(2,1)S(1)} %fusion.68, bf16[8]{0:T(256)(128)(2,1)S(1)} %get-tuple-element.367, s32[8]{0:T(128)S(1)} %dynamic_slice.41), kind=kOutput, calls=%fused_computation.8.clone.1 | convolution fusion | flops 17826304 | bytes 8912944 | tf_op jit(solution)/shard_map/while/body/sd,sir->dir/dot_general | solution.py:46
  52.9 5.1 %convolution_add_fusion.4 = f32[32,128,256]{2,0,1:T(8,128)} fusion(f32[32,128,256]{2,0,1:T(8,128)} %get-tuple-element.392, bf16[8,128,256]{2,1,0:T(8,128)(2,1)S(1)} %fusion.68, bf16[8]{0:T(256)(128)(2,1)S(1)} %get-tuple-element.367, s32[8]{0:T(128)S(1)} %dynamic_slice.41), kind=kOutput, calls=%fused_computation.8.clone.1 | convolution fusion | flops 17826304 | bytes 8912944 | tf_op jit(solution)/shard_map/while/body/sd,sir->dir/dot_general | solution.py:46
  62.3 5.1 %convolution_add_fusion.4 = f32[32,128,256]{2,0,1:T(8,128)} fusion(f32[32,128,256]{2,0,1:T(8,128)} %get-tuple-element.392, bf16[8,128,256]{2,1,0:T(8,128)(2,1)S(1)} %fusion.68, bf16[8]{0:T(256)(128)(2,1)S(1)} %get-tuple-element.367, s32[8]{0:T(128)S(1)} %dynamic_slice.41), kind=kOutput, calls=%fused_computation.8.clone.1 | convolution fusion | flops 17826304 | bytes 8912944 | tf_op jit(solution)/shard_map/while/body/sd,sir->dir/dot_general | solution.py:46
  71.7 5.1 %convolution_add_fusion.4 = f32[32,128,256]{2,0,1:T(8,128)} fusion(f32[32,128,256]{2,0,1:T(8,128)} %get-tuple-element.392, bf16[8,128,256]{2,1,0:T(8,128)(2,1)S(1)} %fusion.68, bf16[8]{0:T(256)(128)(2,1)S(1)} %get-tuple-element.367, s32[8]{0:T(128)S(1)} %dynamic_slice.41), kind=kOutput, calls=%fused_computation.8.clone.1 | convolution fusion | flops 17826304 | bytes 8912944 | tf_op jit(solution)/shard_map/while/body/sd,sir->dir/dot_general | solution.py:46
  81.1 5.1 %convolution_add_fusion.4 = f32[32,128,256]{2,0,1:T(8,128)} fusion(f32[32,128,256]{2,0,1:T(8,128)} %get-tuple-element.392, bf16[8,128,256]{2,1,0:T(8,128)(2,1)S(1)} %fusion.68, bf16[8]{0:T(256)(128)(2,1)S(1)} %get-tuple-element.367, s32[8]{0:T(128)S(1)} %dynamic_slice.41), kind=kOutput, calls=%fused_computation.8.clone.1 | convolution fusion | flops 17826304 | bytes 8912944 | tf_op jit(solution)/shard_map/while/body/sd,sir->dir/dot_general | solution.py:46
  90.5 5.1 %convolution_add_fusion.4 = f32[32,128,256]{2,0,1:T(8,128)} fusion(f32[32,128,256]{2,0,1:T(8,128)} %get-tuple-element.392, bf16[8,128,256]{2,1,0:T(8,128)(2,1)S(1)} %fusion.68, bf16[8]{0:T(256)(128)(2,1)S(1)} %get-tuple-element.367, s32[8]{0:T(128)S(1)} %dynamic_slice.41), kind=kOutput, calls=%fused_computation.8.clone.1 | convolution fusion | flops 17826304 | bytes 8912944 | tf_op jit(solution)/shard_map/while/body/sd,sir->dir/dot_general | solution.py:46
  99.9 5.1 %convolution_add_fusion.4 = f32[32,128,256]{2,0,1:T(8,128)} fusion(f32[32,128,256]{2,0,1:T(8,128)} %get-tuple-element.392, bf16[8,128,256]{2,1,0:T(8,128)(2,1)S(1)} %fusion.68, bf16[8]{0:T(256)(128)(2,1)S(1)} %get-tuple-element.367, s32[8]{0:T(128)S(1)} %dynamic_slice.41), kind=kOutput, calls=%fused_computation.8.clone.1 | convolution fusion | flops 17826304 | bytes 8912944 | tf_op jit(solution)/shard_map/while/body/sd,sir->dir/dot_general | solution.py:46
  109.3 5.1 %convolution_add_fusion.4 = f32[32,128,256]{2,0,1:T(8,128)} fusion(f32[32,128,256]{2,0,1:T(8,128)} %get-tuple-element.392, bf16[8,128,256]{2,1,0:T(8,128)(2,1)S(1)} %fusion.68, bf16[8]{0:T(256)(128)(2,1)S(1)} %get-tuple-element.367, s32[8]{0:T(128)S(1)} %dynamic_slice.41), kind=kOutput, calls=%fused_computation.8.clone.1 | convolution fusion | flops 17826304 | bytes 8912944 | tf_op jit(solution)/shard_map/while/body/sd,sir->dir/dot_general | solution.py:46
  118.7 5.1 %convolution_add_fusion.4 = f32[32,128,256]{2,0,1:T(8,128)} fusion(f32[32,128,256]{2,0,1:T(8,128)} %get-tuple-element.392, bf16[8,128,256]{2,1,0:T(8,128)(2,1)S(1)} %fusion.68, bf16[8]{0:T(256)(128)(2,1)S(1)} %get-tuple-element.367, s32[8]{0:T(128)S(1)} %dynamic_slice.41), kind=kOutput, calls=%fused_computation.8.clone.1 | convolution fusion | flops 17826304 | bytes 8912944 | tf_op jit(solution)/shard_map/while/body/sd,sir->dir/dot_general | solution.py:46
  123.8 6.6 %copy.9 = f32[32,128,256]{2,1,0:T(8,128)} copy(f32[32,128,256]{2,0,1:T(8,128)} %get-tuple-element.112) | data formatting | bytes 8388608 | tf_op jit(solution)/shard_map/while | solution.py:59
  130.4 110.2 %all-reduce.3.cloned.1.call-done = f32[4096,256]{1,0:T(8,128)} async-done(((f32[4096,256]{1,0:T(8,128)}), f32[4096,256]{1,0:T(8,128)}) %all-reduce.3.cloned.1.call-update) | async-done | bytes 4194320 | tf_op jit(solution)/shard_map/psum | solution.py:61
  240.6 10.7 %select_reduce_fusion = (f32[]{:T(128)}, f32[256,256]{1,0:T(8,128)S(1)}) fusion(f32[4096,256]{1,0:T(8,128)} %all-reduce.3.cloned.1.call-done), kind=kOutput, calls=%fused_computation.61 | convolution fusion | flops 3221422080 | bytes 4456452 | tf_op jit(solution)/shard_map/dot_general | solution.py:62
  252.1 11.7 %cholesky.49 = f32[128,128]{1,0:T(8,128)S(1)} custom-call(f32[128,128]{1,0:T(8,128)S(1)} %cholesky.115), custom_call_target="Cholesky" | custom-call | tf_op jit(solution)/shard_map/jit(cholesky)/cholesky | solution.py:18
  263.9 9.8 %custom-call.15 = f32[1,128,128]{1,2,0:T(8,128)S(1)} custom-call(f32[1,128,128]{2,1,0:T(8,128)S(1)} %get-tuple-element.229), custom_call_target="InvertDiagBlocksLowerTriangular" | custom-call | tf_op jit(solution)/shard_map/jit(cholesky)/cholesky | solution.py:18
  274.2 11.7 %cholesky.103 = f32[128,128]{1,0:T(8,128)S(1)} custom-call(f32[128,128]{1,0:T(8,128)S(1)} %convolution_subtract_fusion.1), custom_call_target="Cholesky" | custom-call | tf_op jit(solution)/shard_map/jit(cholesky)/cholesky | solution.py:18
  292.2 19.9 %custom-call.16 = f32[2,128,128]{1,2,0:T(8,128)S(1)} custom-call(f32[2,128,128]{2,1,0:T(8,128)S(1)} %get-tuple-element.121), custom_call_target="InvertDiagBlocksLowerTriangular" | custom-call | tf_op jit(solution)/shard_map/jit(_solve_triangular)/triangular_solve | solution.py:22
  328.4 92.7 %while.25 = (s32[]{:T(128)}, f32[32,128,256]{2,0,1:T(8,128)}, s32[]{:T(128)}, s32[96]{0:T(128)S(1)}, s32[]{:T(128)}, /*index=5*/bf16[96,128,128]{2,1,0:T(8,128)(...) while((s32[]{:T(128)}, f32[32,128,256]{2,0,1:T(8,128)}, ...), condition=%wide.region_9.11_spmd.clone, body=%wide.region_8.10_spmd.clone.sunk | while | flops 85198416 | bytes 11276743 | solution.py:72
  338.8 5.0 %convolution_add_fusion.5 = f32[32,128,256]{2,0,1:T(8,128)} fusion(f32[32,128,256]{2,0,1:T(8,128)} %get-tuple-element.443, bf16[8,128,256]{2,1,0:T(8,128)(2,1)S(1)} %fusion.73, bf16[8]{0:T(256)(128)(2,1)S(1)} %get-tuple-element.378, s32[8]{0:T(128)S(1)} %dynamic_slice.43), kind=kOutput, calls=%fused_computation.29.clone.1 | convolution fusion | flops 17826304 | bytes 8912944 | tf_op jit(solution)/shard_map/while/body/sc,sjr->cjr/dot_general | solution.py:50
  346.5 5.0 %convolution_add_fusion.5 = f32[32,128,256]{2,0,1:T(8,128)} fusion(f32[32,128,256]{2,0,1:T(8,128)} %get-tuple-element.443, bf16[8,128,256]{2,1,0:T(8,128)(2,1)S(1)} %fusion.73, bf16[8]{0:T(256)(128)(2,1)S(1)} %get-tuple-element.378, s32[8]{0:T(128)S(1)} %dynamic_slice.43), kind=kOutput, calls=%fused_computation.29.clone.1 | convolution fusion | flops 17826304 | bytes 8912944 | tf_op jit(solution)/shard_map/while/body/sc,sjr->cjr/dot_general | solution.py:50
  421.0 6.6 %copy.12 = f32[32,128,256]{2,1,0:T(8,128)} copy(f32[32,128,256]{2,0,1:T(8,128)} %get-tuple-element.113) | data formatting | bytes 8388608 | tf_op jit(solution)/shard_map/while | solution.py:72
  (166 shorter events, 163.5 us)
Async XLA Ops:
  6.5 4.5 %copy-start.1 = (s32[96]{0:T(128)S(1)}, s32[96]{0:T(128)}, u32[]{:S(2)}) copy-start(s32[96]{0:T(128)} %param.13) | copy-start | bytes 1156
  6.5 4.5 %copy-start.2 = (s32[96]{0:T(128)S(1)}, s32[96]{0:T(128)}, u32[]{:S(2)}) copy-start(s32[96]{0:T(128)} %param.12) | copy-start | bytes 1156
  6.5 234.1 %all-reduce.3.cloned.1.call-start = ((), (), s32[]{:S(2)}) async-start(), calls=%async_computation | async-start | bytes 8388608 | tf_op jit(solution)/shard_map/psum | solution.py:61
  312.1 3.7 copy-start
Sparse Core Ops, SparseCore 0:
  130.5 110.0 all-reduce.2
where the time goes:
time: 437 us; the launch traced here: 435 us
  matrix products  173 us (40%)
  waiting for transfers between devices  110 us (25%)
  other arithmetic  72.5 us (17%)
  local copies, waits for them, and re-layouts  61.8 us (14%)
  between operations  16.1 us (4%)
    psum x1, waiting for transfers between devices, local(): whole_rows = lax.psum(row_sums, 'term')  110 us
    dot_general x12, matrix products, forward(): return summed + jnp.einsum('sd,sir->dir', one_hot, products)  61.2 us
    dot_general x12, matrix products, backward(): return summed + jnp.einsum('sc,sjr->cjr', one_hot, products)  60.3 us
    another operation x6, other arithmetic, factor(): return jnp.linalg.cholesky(shifted)  34 us
    gather x12, local copies, waits for them, and re-layouts, step_fwd(): jnp.take(q_blocks, cols_now, axis=0)  26.1 us
    another operation x3, other arithmetic, whiten(): jax.scipy.linalg.solve_triangular(chol_lower, row_block.T, lower=True)  19.9 us
    dot_general x12, matrix products, forward(): jnp.einsum('sij,sjr->sir', tiles_now, picked, preferred_element_type=jnp....  15.8 us
    dot_general x12, matrix products, backward(): jnp.einsum('sij,sir->sjr', tiles_now, picked, preferred_element_type=jnp....  15.8 us
  transfers between devices with their start and end apart: 1, of which 1 were waited for; matrix products, arithmetic and copies ran while one was open for 0% of the time, Pallas kernels for 0%

commit v1 on v0

v1 whole, which is shorter than its diff:
```python
import functools

import jax
import jax.numpy as jnp
from jax import lax
from jax.experimental import pallas as pl
from jax.experimental.pallas import tpu as pltpu
from jax.sharding import PartitionSpec as P

DOC_BLKS = 32
GROUP = 4
MIB = 1024 * 1024

shift_ratio = 0.001


def each_slot(count, body):
    whole = count // GROUP

    def group(index, carry):
        body([index * GROUP + k for k in range(GROUP)])
        return carry

    def single(index, carry):
        body([index])
        return carry

    lax.fori_loop(0, whole, group, 0)
    lax.fori_loop(whole * GROUP, count, single, 0)


def forward_kernel(count_ref, doc_ref, col_ref, tiles_ref, panel_ref, rows_ref, total):
    tile = tiles_ref.shape[1]
    count = count_ref[lax.axis_index("term")]
    total[...] = jnp.zeros_like(total)

    def body(slots):
        products = []
        for slot in slots:
            start = pl.multiple_of(col_ref[slot] * tile, tile)
            products.append(
                jnp.dot(
                    tiles_ref[slot],
                    panel_ref[pl.ds(start, tile), :],
                    preferred_element_type=jnp.float32,
                )
            )
        for slot, product in zip(slots, products):
            start = pl.multiple_of(doc_ref[slot] * tile, tile)
            total[pl.ds(start, tile), :] += product

    each_slot(count, body)
    rows_ref[...] = total[...].astype(rows_ref.dtype)


def exchange_kernel(n, chunks, orders, x_ref, y_ref, *scratch):
    stages = len(orders[0])
    recv_bufs = scratch[:stages]
    send_bufs = scratch[stages : 2 * stages - 1]
    keep_bufs = scratch[2 * stages - 1 : 3 * stages - 2]
    send_sems, recv_sems = scratch[3 * stages - 2 :]
    me = lax.axis_index("term")
    rows = x_ref.shape[0] // chunks

    def bit_of(bit):
        return (me // (1 << bit)) % 2

    def partner(bit):
        return me + (1 << bit) - 2 * (1 << bit) * bit_of(bit)

    barrier = pltpu.get_barrier_semaphore()
    for bit in range(stages):
        pl.semaphore_signal(
            barrier, inc=1, device_id={"term": partner(bit)}, device_id_type=pl.DeviceIdType.MESH
        )
    pl.semaphore_wait(barrier, stages)

    started = []

    def send(phase, stage, chunk, bit, src, dst):
        copy = pltpu.make_async_remote_copy(
            src_ref=src,
            dst_ref=dst,
            send_sem=send_sems.at[phase, stage, chunk],
            recv_sem=recv_sems.at[phase, stage, chunk],
            device_id={"term": partner(bit)},
            device_id_type=pl.DeviceIdType.MESH,
        )
        copy.start()
        started.append(copy)
        return copy

    offsets = [[None] * (stages + 1) for _ in range(chunks)]
    reduce_copies = [[None] * stages for _ in range(chunks)]
    for chunk in range(chunks):
        offset = chunk * rows
        offsets[chunk][0] = offset
        for stage, bit in enumerate(orders[chunk]):
            half = rows >> (stage + 1)
            offset = offset + bit_of(bit) * half
            offsets[chunk][stage + 1] = offset
        half = rows // 2
        bit = orders[chunk][0]
        away = pl.multiple_of(chunk * rows + (1 - bit_of(bit)) * half, 16)
        reduce_copies[chunk][0] = send(
            0, 0, chunk, bit, x_ref.at[pl.ds(away, half)], recv_bufs[0].at[chunk]
        )

    def add_into(count, dst, dst_at, left, left_at, right, right_at):
        step = min(count, 64)

        def piece(index, carry):
            at = index * step

            def where(base):
                return pl.ds(pl.multiple_of(base + at, 16), step)

            value = left[where(left_at), :].astype(jnp.float32) + right[where(right_at), :].astype(
                jnp.float32
            )
            dst[where(dst_at), :] = value.astype(dst.dtype)
            return carry

        lax.fori_loop(0, count // step, piece, 0)

    gather_copies = [[None] * stages for _ in range(chunks)]

    def start_gather(chunk, stage):
        size = rows >> (stage + 1)
        at = pl.multiple_of(offsets[chunk][stage + 1], 16)
        block = y_ref.at[pl.ds(at, size)]
        gather_copies[chunk][stage] = send(1, stage, chunk, orders[chunk][stage], block, block)

    for stage in range(stages):
        size = rows >> (stage + 1)
        for chunk in range(chunks):
            reduce_copies[chunk][stage].wait_recv()
            got = recv_bufs[stage].at[chunk]
            if stage == 0:
                held, held_at = x_ref, offsets[chunk][1]
            else:
                held, held_at = keep_bufs[stage - 1].at[chunk], 0
            if stage == stages - 1:
                add_into(size, y_ref, offsets[chunk][stages], held, held_at, got, 0)
                start_gather(chunk, stage)
            else:
                bit = orders[chunk][stage + 1]
                half = size // 2
                mine, other = bit_of(bit) * half, (1 - bit_of(bit)) * half
                out = send_bufs[stage].at[chunk]
                add_into(half, out, 0, held, held_at + other, got, other)
                reduce_copies[chunk][stage + 1] = send(
                    0, stage + 1, chunk, bit, out, recv_bufs[stage + 1].at[chunk]
                )
                add_into(half, keep_bufs[stage].at[chunk], 0, held, held_at + mine, got, mine)

    for stage in reversed(range(stages)):
        for chunk in range(chunks):
            gather_copies[chunk][stage].wait_recv()
            if stage > 0:
                start_gather(chunk, stage - 1)
    for copy in started:
        copy.wait_send()


def dot32(a, b, dims):
    return lax.dot_general(
        a, b, (dims, ((), ())), precision=lax.Precision.HIGHEST, preferred_element_type=jnp.float32
    )


def backward_kernel(
    count_ref, doc_ref, col_ref, tiles_ref, rows_ref, out_ref, ortho, inverse, matrix
):
    tile = tiles_ref.shape[1]
    rank = rows_ref.shape[1]
    count = count_ref[lax.axis_index("term")]
    depth = 512
    matrix[...] = jnp.zeros_like(matrix)

    def gram_step(index, carry):
        block = rows_ref[pl.ds(pl.multiple_of(index * depth, depth), depth), :]
        matrix[...] += lax.dot_general(
            block, block, (((0,), (0,)), ((), ())), preferred_element_type=jnp.float32
        )
        return carry

    lax.fori_loop(0, rows_ref.shape[0] // depth, gram_step, 0)
    row_ids = lax.broadcasted_iota(jnp.int32, (rank, rank), 0)
    lane_ids = lax.broadcasted_iota(jnp.int32, (rank, rank), 1)
    eye = (row_ids == lane_ids).astype(jnp.float32)
    gram = matrix[...]
    shift = shift_ratio * jnp.sum(gram * eye) / rank
    gram = gram + shift * eye
    scale_row = lax.rsqrt(jnp.sum(gram * eye, axis=0, keepdims=True))
    scale_col = lax.rsqrt(jnp.sum(gram * eye, axis=1, keepdims=True))
    gram = gram * scale_row * scale_col
    matrix[...] = gram
    inverse[...] = eye
    half_lower = jnp.where(row_ids > lane_ids, 1.0, jnp.where(row_ids == lane_ids, 0.5, 0.0))

    def unsolved(state):
        index, error = state
        return jnp.logical_and(index < 12, jnp.logical_not(error < 1e-6))

    def newton(state):
        index, _ = state
        now = inverse[...]
        left = dot32(now, matrix[...], ((1,), (0,)))
        gap = dot32(left, now, ((1,), (1,))) - eye
        inverse[...] = now - dot32(gap * half_lower, now, ((1,), (0,)))
        return index + 1, jnp.sum(gap * gap)

    _, error = lax.while_loop(unsolved, newton, (0, jnp.float32(1e30)))

    @pl.when(jnp.logical_not(error < 1e-6))
    def _():
        inverse[...] = eye
        lanes = lax.broadcasted_iota(jnp.int32, (1, rank), 1)

        def column(index, carry):
            pivot_row = matrix[pl.ds(index, 1), :]
            pivot = jnp.sum(jnp.where(lanes == index, pivot_row, 0.0), axis=1, keepdims=True)
            root = lax.rsqrt(pivot)
            factors = jnp.sum(
                jnp.where(lane_ids == index, matrix[...], 0.0), axis=1, keepdims=True
            )
            factors = jnp.where(row_ids[:, :1] > index, factors * root, 0.0)
            solved = inverse[pl.ds(index, 1), :] * root
            matrix[...] -= factors * (pivot_row * root)
            inverse[...] -= factors * solved
            inverse[pl.ds(index, 1), :] = solved
            return carry

        lax.fori_loop(0, rank, column, 0)

    whitener = (inverse[...] * scale_row).astype(jnp.bfloat16)

    def whiten_step(index, carry):
        where = pl.ds(pl.multiple_of(index * depth, depth), depth)
        ortho[where, :] = lax.dot_general(
            rows_ref[where, :],
            whitener,
            (((1,), (1,)), ((), ())),
            preferred_element_type=jnp.float32,
        ).astype(jnp.bfloat16)
        return carry

    lax.fori_loop(0, rows_ref.shape[0] // depth, whiten_step, 0)
    out_ref[...] = jnp.zeros_like(out_ref)

    def body(slots):
        products = []
        for slot in slots:
            start = pl.multiple_of(doc_ref[slot] * tile, tile)
            products.append(
                lax.dot_general(
                    tiles_ref[slot],
                    ortho[pl.ds(start, tile), :],
                    (((0,), (0,)), ((), ())),
                    preferred_element_type=jnp.float32,
                )
            )
        for slot, product in zip(slots, products):
            start = pl.multiple_of(col_ref[slot] * tile, tile)
            out_ref[pl.ds(start, tile), :] += product

    each_slot(count, body)


def exchange(rows, n):
    bits = n.bit_length() - 1
    height, rank = rows.shape
    chunks = max(1, min(4, height // (16 * n)))
    plain = list(range(bits))
    swapped = [0, 2, 1] + plain[3:] if bits > 2 else plain
    orders = [swapped if chunk == chunks - 1 and chunks > 1 else plain for chunk in range(chunks)]
    size = height // chunks
    scratch = [pltpu.VMEM((chunks, size >> (k + 1), rank), jnp.bfloat16) for k in range(bits)]
    scratch += [pltpu.VMEM((chunks, size >> (k + 2), rank), jnp.bfloat16) for k in range(bits - 1)]
    scratch += [pltpu.VMEM((chunks, size >> (k + 2), rank), jnp.float32) for k in range(bits - 1)]
    scratch += [pltpu.SemaphoreType.DMA((2, bits, chunks))] * 2
    return pl.pallas_call(
        functools.partial(exchange_kernel, n, chunks, orders),
        out_shape=jax.ShapeDtypeStruct(rows.shape, jnp.bfloat16),
        in_specs=[pl.BlockSpec(memory_space=pltpu.VMEM)],
        out_specs=pl.BlockSpec(memory_space=pltpu.VMEM),
        scratch_shapes=scratch,
        compiler_params=pltpu.CompilerParams(
            collective_id=0, has_side_effects=True, vmem_limit_bytes=40 * MIB
        ),
        name="exchange",
    )(rows)


def local(n, tile_values, tile_doc, tile_col, tile_count, panel):
    tile = tile_values.shape[1]
    rank = panel.shape[1]
    height = DOC_BLKS * tile
    smem = pl.BlockSpec(memory_space=pltpu.SMEM)
    vmem = pl.BlockSpec(memory_space=pltpu.VMEM)
    params = pltpu.CompilerParams(vmem_limit_bytes=40 * MIB)
    rows = pl.pallas_call(
        forward_kernel,
        out_shape=jax.ShapeDtypeStruct((height, rank), jnp.bfloat16),
        in_specs=[smem, smem, smem, vmem, vmem],
        out_specs=vmem,
        scratch_shapes=[pltpu.VMEM((height, rank), jnp.float32)],
        compiler_params=params,
        name="forward",
    )(tile_count, tile_doc, tile_col, tile_values, panel)
    rows = exchange(rows, n)
    return pl.pallas_call(
        backward_kernel,
        out_shape=jax.ShapeDtypeStruct(panel.shape, jnp.float32),
        in_specs=[smem, smem, smem, vmem, vmem],
        out_specs=vmem,
        scratch_shapes=[
            pltpu.VMEM((height, rank), jnp.bfloat16),
            pltpu.VMEM((rank, rank), jnp.float32),
            pltpu.VMEM((rank, rank), jnp.float32),
        ],
        compiler_params=params,
        name="backward",
    )(tile_count, tile_doc, tile_col, tile_values, rows)


def solution(mesh):
    return jax.shard_map(
        functools.partial(local, mesh.shape["term"]),
        mesh=mesh,
        in_specs=(
            P(("dom", "term"), None, None),
            P(("dom", "term")),
            P(("dom", "term")),
            P("dom"),
            P("term", None),
        ),
        out_specs=P(("dom", "term"), None),
        check_vma=False,
    )
```

time: 437 us -> 121 us (0.28)
  matrix products: 173 us -> 0 us
  Pallas kernels: 0 us -> 115 us
  waiting for transfers between devices: 110 us -> 0 us
  other arithmetic: 72.5 us -> 0 us
  local copies, waits for them, and re-layouts: 61.8 us -> 5.45 us
  between operations: 16.1 us -> 0.04 us
    dot_general x49 -> x0, matrix products: 164 us -> none  [the longest x12 61.2 us: forward(): return summed + jnp.einsum('sd,sir->dir', one_hot, products)]
    pallas_call x0 -> x3, Pallas kernels: none -> 115 us  [the longest x1 67.8 us: local(): pl.pallas_call(backward_kernel, out_shape=jax.ShapeDtypeStruct(panel.shap...]
    psum x1 -> x0, waiting for transfers between devices: 110 us -> none  [local(): whole_rows = lax.psum(row_sums, 'term')]
    another operation x9 -> x0, other arithmetic: 54 us -> none  [the longest x6 34 us: factor(): return jnp.linalg.cholesky(shifted)]
    gather x24 -> x0, local copies, waits for them, and re-layouts: 33 us -> none  [the longest x12 26.1 us: step_fwd(): jnp.take(q_blocks, cols_now, axis=0)]
    and x24 -> x0, other arithmetic: 16.9 us -> none  [the longest x12 8.47 us: step_fwd(): jnp.take(q_blocks, cols_now, axis=0)]
    while x2 -> x0, local copies, waits for them, and re-layouts: 13.2 us -> none  [the longest x1 6.63 us: local(): lax.fori_loop(0, (own_count + block_slots - 1) // block_slots, step_bwd,...]
    another operation x5 -> x0, matrix products: 9.53 us -> none  [the longest x3 9.06 us: whiten(): jax.scipy.linalg.solve_triangular(chol_lower, row_block.T, lower=True)]
  transfers between devices with their start and end apart: 1 -> 0, of which waited for: 1 -> 0; matrix products, arithmetic and copies ran while one was open for 0% -> 0% of each run, Pallas kernels for 0% -> 0%
where the time goes in v1:
time: 121 us
  Pallas kernels  115 us (95%)
  local copies, waits for them, and re-layouts  5.45 us (5%)
    pallas_call x1, Pallas kernels, local(): pl.pallas_call(backward_kernel, out_shape=jax.ShapeDtypeStruct(panel.shap...  67.8 us
    pallas_call x1, Pallas kernels, exchange(): pl.pallas_call(functools.partial(exchange_kernel, n, chunks, orders), out...  40.8 us
    pallas_call x1, Pallas kernels, local(): pl.pallas_call(forward_kernel, out_shape=jax.ShapeDtypeStruct((height, ra...  6.55 us
    unnamed x12, local copies, waits for them, and re-layouts  5.45 us

profile of v1, /device:TPU:0, one launch (start us, length us, event | category | flops | bytes accessed | tf_op | source)
XLA Modules:
  0.0 120.6 jit_solution(16252587099572642536)
XLA Ops:
  0.0 0.0 copy-start
  0.0 1.9 %copy-done = bf16[96,128,128]{2,1,0:T(8,128)(2,1)S(1)} copy-done((bf16[96,128,128]{2,1,0:T(8,128)(2,1)S(1)}, bf16[96,128,128]{2,1,0:T(8,128)(2,1)}, u32[]{:S(2)}) %copy-start) | copy-done | bytes 3145752
  1.9 0.0 copy-start.2
  1.9 1.6 %copy-done.2 = bf16[4096,256]{1,0:T(8,128)(2,1)S(1)} copy-done((bf16[4096,256]{1,0:T(8,128)(2,1)S(1)}, bf16[4096,256]{1,0:T(8,128)(2,1)}, u32[]{:S(2)}) %copy-start.2) | copy-done | bytes 2097176
  3.5 0.0 copy-start.3
  3.5 0.7 copy-done.3
  4.1 0.0 copy-start.4
  4.1 0.7 copy-done.4
  4.8 0.0 copy-start.5
  4.8 0.7 copy-done.5
  5.4 6.5 %forward.1.x_ref = bf16[4096,256]{1,0:T(8,128)(2,1)S(1)} custom-call(s32[16]{0:T(128)S(1)} %copy-done.3, s32[96]{0:T(128)S(1)} %copy-done.4, s32[96]{0:T(128)S(1)} %copy-done.5, bf16[96,128,128]{2,1,0:T(8,128)(2,1)S(1)} %copy-done, bf16[4096,256]{1,0:T(8,128)(2,1)S(1)} %copy-done.2), custom_call_target="tpu_custom_call" | custom-call | tf_op jit(solution)/shard_map/forward/pallas_call | solution.py:303
  12.0 0.0 copy-start.1
  12.0 40.8 %exchange.1.rows_ref = bf16[4096,256]{1,0:T(8,128)(2,1)S(1)} custom-call(bf16[4096,256]{1,0:T(8,128)(2,1)S(1)} %forward.1.x_ref), custom_call_target="tpu_custom_call" | custom-call | tf_op jit(solution)/shard_map/exchange/pallas_call | solution.py:283
  52.8 0.0 copy-done.1
  52.8 67.8 %backward.1 = f32[4096,256]{1,0:T(8,128)} custom-call(s32[16]{0:T(128)S(1)} %copy-done.3, s32[96]{0:T(128)S(1)} %copy-done.4, s32[96]{0:T(128)S(1)} %copy-done.5, bf16[96,128,128]{2,1,0:T(8,128)(2,1)S(1)} %copy-done.1, bf16[4096,256]{1,0:T(8,128)(2,1)S(1)} %exchange.1.rows_ref), custom_call_target="tpu_custom_call" | custom-call | tf_op jit(solution)/shard_map/backward/pallas_call | solution.py:313
Async XLA Ops:
  0.0 1.9 %copy-start = (bf16[96,128,128]{2,1,0:T(8,128)(2,1)S(1)}, bf16[96,128,128]{2,1,0:T(8,128)(2,1)}, u32[]{:S(2)}) copy-start(bf16[96,128,128]{2,1,0:T(8,128)(2,1)} %tiles_ref.3) | copy-start | bytes 9437188
  1.9 1.6 %copy-start.2 = (bf16[4096,256]{1,0:T(8,128)(2,1)S(1)}, bf16[4096,256]{1,0:T(8,128)(2,1)}, u32[]{:S(2)}) copy-start(bf16[4096,256]{1,0:T(8,128)(2,1)} %panel_ref.1) | copy-start | bytes 6291460
  3.5 0.7 copy-start.3
  4.1 0.7 copy-start.4
  4.8 0.7 copy-start.5
  12.0 40.8 %copy-start.1 = (bf16[96,128,128]{2,1,0:T(8,128)(2,1)S(1)}, bf16[96,128,128]{2,1,0:T(8,128)(2,1)}, u32[]{:S(2)}) copy-start(bf16[96,128,128]{2,1,0:T(8,128)(2,1)} %tiles_ref.3) | copy-start | bytes 9437188

commit v2 on v1

--- a/solution.py
+++ b/solution.py
@@ -8,7 +8,7 @@
 from jax.sharding import PartitionSpec as P
 
 DOC_BLKS = 32
-GROUP = 4
+GROUP = 8
 MIB = 1024 * 1024
 
 shift_ratio = 0.001
@@ -29,10 +29,30 @@
     lax.fori_loop(whole * GROUP, count, single, 0)
 
 
-def forward_kernel(count_ref, doc_ref, col_ref, tiles_ref, panel_ref, rows_ref, total):
+def start_copies(sources, targets, sems):
+    copies = [
+        pltpu.make_async_copy(source, target, sems.at[index])
+        for index, (source, target) in enumerate(zip(sources, targets))
+    ]
+    for copy in copies:
+        copy.start()
+    return copies
+
+
+def forward_kernel(
+    count_hbm, doc_hbm, col_hbm, tiles_hbm, panel_hbm, rows_ref,
+    count_ref, doc_ref, col_ref, tiles_ref, panel_ref, total, sems,
+):
     tile = tiles_ref.shape[1]
+    copies = start_copies(
+        (count_hbm, doc_hbm, col_hbm, panel_hbm, tiles_hbm),
+        (count_ref, doc_ref, col_ref, panel_ref, tiles_ref),
+        sems,
+    )
+    total[...] = jnp.zeros_like(total)
+    for copy in copies:
+        copy.wait()
     count = count_ref[lax.axis_index("term")]
-    total[...] = jnp.zeros_like(total)
 
     def body(slots):
         products = []
@@ -53,7 +73,7 @@
     rows_ref[...] = total[...].astype(rows_ref.dtype)
 
 
-def exchange_kernel(n, chunks, orders, x_ref, y_ref, *scratch):
+def exchange_kernel(chunks, orders, x_ref, y_ref, gram_ref, *scratch):
     stages = len(orders[0])
     recv_bufs = scratch[:stages]
     send_bufs = scratch[stages : 2 * stages - 1]
@@ -62,18 +82,24 @@
     me = lax.axis_index("term")
     rows = x_ref.shape[0] // chunks
 
+    def width(bit):
+        if isinstance(bit, tuple):
+            return (1 << bit[0]) + ((1 << bit[1]) - (1 << bit[0])) * (me % 2)
+        return 1 << bit
+
     def bit_of(bit):
-        return (me // (1 << bit)) % 2
+        return (me // width(bit)) % 2
 
     def partner(bit):
-        return me + (1 << bit) - 2 * (1 << bit) * bit_of(bit)
+        return me + width(bit) - 2 * width(bit) * bit_of(bit)
 
     barrier = pltpu.get_barrier_semaphore()
-    for bit in range(stages):
+    bits = list(dict.fromkeys(bit for order in orders for bit in order))
+    for bit in bits:
         pl.semaphore_signal(
             barrier, inc=1, device_id={"term": partner(bit)}, device_id_type=pl.DeviceIdType.MESH
         )
-    pl.semaphore_wait(barrier, stages)
+    pl.semaphore_wait(barrier, len(bits))
 
     started = []
 
@@ -131,36 +157,58 @@
         block = y_ref.at[pl.ds(at, size)]
         gather_copies[chunk][stage] = send(1, stage, chunk, orders[chunk][stage], block, block)
 
-    for stage in range(stages):
+    def reduce_step(stage, chunk):
         size = rows >> (stage + 1)
+        reduce_copies[chunk][stage].wait_recv()
+        got = recv_bufs[stage].at[chunk]
+        if stage == 0:
+            held, held_at = x_ref, offsets[chunk][1]
+        else:
+            held, held_at = keep_bufs[stage - 1].at[chunk], 0
+        if stage == stages - 1:
+            add_into(size, y_ref, offsets[chunk][stages], held, held_at, got, 0)
+            start_gather(chunk, stage)
+        else:
+            bit = orders[chunk][stage + 1]
+            half = size // 2
+            mine, other = bit_of(bit) * half, (1 - bit_of(bit)) * half
+            out = send_bufs[stage].at[chunk]
+            add_into(half, out, 0, held, held_at + other, got, other)
+            reduce_copies[chunk][stage + 1] = send(
+                0, stage + 1, chunk, bit, out, recv_bufs[stage + 1].at[chunk]
+            )
+            add_into(half, keep_bufs[stage].at[chunk], 0, held, held_at + mine, got, mine)
+
+    gram_ref[...] = jnp.zeros_like(gram_ref)
+
+    def gather_step(stage, chunk):
+        gather_copies[chunk][stage].wait_recv()
+        if stage > 0:
+            start_gather(chunk, stage - 1)
+        else:
+            block = y_ref[chunk * rows : (chunk + 1) * rows, :]
+            gram_ref[...] += lax.dot_general(
+                block, block, (((0,), (0,)), ((), ())), preferred_element_type=jnp.float32
+            )
+
+    for diagonal in range(2 * stages + chunks - 1):
         for chunk in range(chunks):
-            reduce_copies[chunk][stage].wait_recv()
-            got = recv_bufs[stage].at[chunk]
-            if stage == 0:
-                held, held_at = x_ref, offsets[chunk][1]
-            else:
-                held, held_at = keep_bufs[stage - 1].at[chunk], 0
-            if stage == stages - 1:
-                add_into(size, y_ref, offsets[chunk][stages], held, held_at, got, 0)
-                start_gather(chunk, stage)
-            else:
-                bit = orders[chunk][stage + 1]
-                half = size // 2
-                mine, other = bit_of(bit) * half, (1 - bit_of(bit)) * half
-                out = send_bufs[stage].at[chunk]
-                add_into(half, out, 0, held, held_at + other, got, other)
-                reduce_copies[chunk][stage + 1] = send(
-                    0, stage + 1, chunk, bit, out, recv_bufs[stage + 1].at[chunk]
-                )
-                add_into(half, keep_bufs[stage].at[chunk], 0, held, held_at + mine, got, mine)
-
-    for stage in reversed(range(stages)):
-        for chunk in range(chunks):
-            gather_copies[chunk][stage].wait_recv()
-            if stage > 0:
-                start_gather(chunk, stage - 1)
+            step = diagonal - chunk
+            if 0 <= step < stages:
+                reduce_step(step, chunk)
+            elif stages <= step < 2 * stages:
+                gather_step(2 * stages - 1 - step, chunk)
     for copy in started:
         copy.wait_send()
+
+
+def dot16(a, b, dims):
+    return lax.dot_general(
+        a.astype(jnp.bfloat16),
+        b.astype(jnp.bfloat16),
+        (dims, ((), ())),
+        preferred_element_type=jnp.float32,
+    )
 
 
 def dot32(a, b, dims):
@@ -170,26 +218,20 @@
 
 
 def backward_kernel(
-    count_ref, doc_ref, col_ref, tiles_ref, rows_ref, out_ref, ortho, inverse, matrix
+    count_hbm, doc_hbm, col_hbm, tiles_hbm, rows_ref, gram_ref, out_ref,
+    count_ref, doc_ref, col_ref, tiles_ref, ortho, inverse, matrix, sems,
 ):
     tile = tiles_ref.shape[1]
     rank = rows_ref.shape[1]
-    count = count_ref[lax.axis_index("term")]
     depth = 512
-    matrix[...] = jnp.zeros_like(matrix)
-
-    def gram_step(index, carry):
-        block = rows_ref[pl.ds(pl.multiple_of(index * depth, depth), depth), :]
-        matrix[...] += lax.dot_general(
-            block, block, (((0,), (0,)), ((), ())), preferred_element_type=jnp.float32
-        )
-        return carry
-
-    lax.fori_loop(0, rows_ref.shape[0] // depth, gram_step, 0)
+    copies = start_copies(
+        (count_hbm, doc_hbm, col_hbm, tiles_hbm), (count_ref, doc_ref, col_ref, tiles_ref), sems
+    )
+    out_ref[...] = jnp.zeros_like(out_ref)
     row_ids = lax.broadcasted_iota(jnp.int32, (rank, rank), 0)
     lane_ids = lax.broadcasted_iota(jnp.int32, (rank, rank), 1)
     eye = (row_ids == lane_ids).astype(jnp.float32)
-    gram = matrix[...]
+    gram = gram_ref[...]
     shift = shift_ratio * jnp.sum(gram * eye) / rank
     gram = gram + shift * eye
     scale_row = lax.rsqrt(jnp.sum(gram * eye, axis=0, keepdims=True))
@@ -199,21 +241,26 @@
     inverse[...] = eye
     half_lower = jnp.where(row_ids > lane_ids, 1.0, jnp.where(row_ids == lane_ids, 0.5, 0.0))
 
-    def unsolved(state):
-        index, error = state
-        return jnp.logical_and(index < 12, jnp.logical_not(error < 1e-6))
-
-    def newton(state):
-        index, _ = state
-        now = inverse[...]
-        left = dot32(now, matrix[...], ((1,), (0,)))
-        gap = dot32(left, now, ((1,), (1,))) - eye
-        inverse[...] = now - dot32(gap * half_lower, now, ((1,), (0,)))
-        return index + 1, jnp.sum(gap * gap)
-
-    _, error = lax.while_loop(unsolved, newton, (0, jnp.float32(1e30)))
-
-    @pl.when(jnp.logical_not(error < 1e-6))
+    def newton(most, goal, dot):
+        def unsolved(state):
+            index, error = state
+            return jnp.logical_and(index < most, jnp.logical_not(error < goal))
+
+        def step(state):
+            index, _ = state
+            now = inverse[...]
+            left = dot(now, matrix[...], ((1,), (0,)))
+            gap = dot(left, now, ((1,), (1,))) - eye
+            inverse[...] = now - dot(gap * half_lower, now, ((1,), (0,)))
+            return index + 1, jnp.sum(gap * gap)
+
+        _, error = lax.while_loop(unsolved, step, (0, jnp.float32(1e30)))
+        return error
+
+    newton(6, 0.1, dot16)
+    error = newton(12, 1e-4, dot32)
+
+    @pl.when(jnp.logical_not(error < 1e-4))
     def _():
         inverse[...] = eye
         lanes = lax.broadcasted_iota(jnp.int32, (1, rank), 1)
@@ -247,7 +294,9 @@
         return carry
 
     lax.fori_loop(0, rows_ref.shape[0] // depth, whiten_step, 0)
-    out_ref[...] = jnp.zeros_like(out_ref)
+    for copy in copies:
+        copy.wait()
+    count = count_ref[lax.axis_index("term")]
 
     def body(slots):
         products = []
@@ -268,23 +317,28 @@
     each_slot(count, body)
 
 
-def exchange(rows, n):
+def orders_of(n, height):
     bits = n.bit_length() - 1
+    order = [0, (2, 1), (1, 2)] + list(range(3, bits)) if bits > 2 else list(range(bits))
+    return [order] * max(1, min(4, height // (16 * n)))
+
+
+def exchange(rows, orders):
     height, rank = rows.shape
-    chunks = max(1, min(4, height // (16 * n)))
-    plain = list(range(bits))
-    swapped = [0, 2, 1] + plain[3:] if bits > 2 else plain
-    orders = [swapped if chunk == chunks - 1 and chunks > 1 else plain for chunk in range(chunks)]
+    chunks, bits = len(orders), len(orders[0])
     size = height // chunks
     scratch = [pltpu.VMEM((chunks, size >> (k + 1), rank), jnp.bfloat16) for k in range(bits)]
     scratch += [pltpu.VMEM((chunks, size >> (k + 2), rank), jnp.bfloat16) for k in range(bits - 1)]
     scratch += [pltpu.VMEM((chunks, size >> (k + 2), rank), jnp.float32) for k in range(bits - 1)]
     scratch += [pltpu.SemaphoreType.DMA((2, bits, chunks))] * 2
     return pl.pallas_call(
-        functools.partial(exchange_kernel, n, chunks, orders),
-        out_shape=jax.ShapeDtypeStruct(rows.shape, jnp.bfloat16),
+        functools.partial(exchange_kernel, chunks, orders),
+        out_shape=(
+            jax.ShapeDtypeStruct(rows.shape, jnp.bfloat16),
+            jax.ShapeDtypeStruct((rank, rank), jnp.float32),
+        ),
         in_specs=[pl.BlockSpec(memory_space=pltpu.VMEM)],
-        out_specs=pl.BlockSpec(memory_space=pltpu.VMEM),
+        out_specs=(pl.BlockSpec(memory_space=pltpu.VMEM),) * 2,
         scratch_shapes=scratch,
         compiler_params=pltpu.CompilerParams(
             collective_id=0, has_side_effects=True, vmem_limit_bytes=40 * MIB
@@ -297,32 +351,45 @@
     tile = tile_values.shape[1]
     rank = panel.shape[1]
     height = DOC_BLKS * tile
-    smem = pl.BlockSpec(memory_space=pltpu.SMEM)
+    hbm = pl.BlockSpec(memory_space=pltpu.HBM)
     vmem = pl.BlockSpec(memory_space=pltpu.VMEM)
     params = pltpu.CompilerParams(vmem_limit_bytes=40 * MIB)
+    slots = [
+        pltpu.SMEM(tile_count.shape, jnp.int32),
+        pltpu.SMEM(tile_doc.shape, jnp.int32),
+        pltpu.SMEM(tile_col.shape, jnp.int32),
+        pltpu.VMEM(tile_values.shape, jnp.bfloat16),
+    ]
     rows = pl.pallas_call(
         forward_kernel,
         out_shape=jax.ShapeDtypeStruct((height, rank), jnp.bfloat16),
-        in_specs=[smem, smem, smem, vmem, vmem],
+        in_specs=[hbm] * 5,
         out_specs=vmem,
-        scratch_shapes=[pltpu.VMEM((height, rank), jnp.float32)],
+        scratch_shapes=slots
+        + [
+            pltpu.VMEM(panel.shape, jnp.bfloat16),
+            pltpu.VMEM((height, rank), jnp.float32),
+            pltpu.SemaphoreType.DMA((5,)),
+        ],
         compiler_params=params,
         name="forward",
     )(tile_count, tile_doc, tile_col, tile_values, panel)
-    rows = exchange(rows, n)
+    rows, gram = exchange(rows, orders_of(n, height))
     return pl.pallas_call(
         backward_kernel,
         out_shape=jax.ShapeDtypeStruct(panel.shape, jnp.float32),
-        in_specs=[smem, smem, smem, vmem, vmem],
+        in_specs=[hbm] * 4 + [vmem] * 2,
         out_specs=vmem,
-        scratch_shapes=[
+        scratch_shapes=slots
+        + [
             pltpu.VMEM((height, rank), jnp.bfloat16),
             pltpu.VMEM((rank, rank), jnp.float32),
             pltpu.VMEM((rank, rank), jnp.float32),
+            pltpu.SemaphoreType.DMA((4,)),
         ],
         compiler_params=params,
         name="backward",
-    )(tile_count, tile_doc, tile_col, tile_values, rows)
+    )(tile_count, tile_doc, tile_col, tile_values, rows, gram)
 
 
 def solution(mesh):

time: 121 us -> 119 us (0.983)
    pallas_call x1, Pallas kernels: 40.8 us -> 43.4 us  [exchange(): pl.pallas_call(functools.partial(exchange_kernel, chunks, orders), out_sh...]
    pallas_call x1, Pallas kernels: 67.8 us -> 65.6 us  [local(): pl.pallas_call(backward_kernel, out_shape=jax.ShapeDtypeStruct(panel.shap...]
    pallas_call x1, Pallas kernels: 6.55 us -> 4.5 us  [local(): pl.pallas_call(forward_kernel, out_shape=jax.ShapeDtypeStruct((height, ra...]
where the time goes in v2:
time: 119 us
  Pallas kernels  114 us (96%)
  local copies, waits for them, and re-layouts  5.45 us (5%)
    pallas_call x1, Pallas kernels, local(): pl.pallas_call(backward_kernel, out_shape=jax.ShapeDtypeStruct(panel.shap...  65.6 us
    pallas_call x1, Pallas kernels, exchange(): pl.pallas_call(functools.partial(exchange_kernel, chunks, orders), out_sh...  43.4 us
    unnamed x12, local copies, waits for them, and re-layouts  5.45 us
    pallas_call x1, Pallas kernels, local(): pl.pallas_call(forward_kernel, out_shape=jax.ShapeDtypeStruct((height, ra...  4.5 us

profile of v2, /device:TPU:0, one launch (start us, length us, event | category | flops | bytes accessed | tf_op | source)
XLA Modules:
  0.0 119.1 jit_solution(10079660882713997605)
XLA Ops:
  0.0 0.0 copy-start
  0.0 1.9 %copy-done = bf16[96,128,128]{2,1,0:T(8,128)(2,1)S(1)} copy-done((bf16[96,128,128]{2,1,0:T(8,128)(2,1)S(1)}, bf16[96,128,128]{2,1,0:T(8,128)(2,1)}, u32[]{:S(2)}) %copy-start) | copy-done | bytes 3145752
  1.9 0.0 copy-start.2
  1.9 1.6 %copy-done.2 = bf16[4096,256]{1,0:T(8,128)(2,1)S(1)} copy-done((bf16[4096,256]{1,0:T(8,128)(2,1)S(1)}, bf16[4096,256]{1,0:T(8,128)(2,1)}, u32[]{:S(2)}) %copy-start.2) | copy-done | bytes 2097176
  3.5 0.0 copy-start.3
  3.5 0.7 copy-done.3
  4.1 0.0 copy-start.4
  4.1 0.7 copy-done.4
  4.8 0.0 copy-start.5
  4.8 0.7 copy-done.5
  5.4 0.0 copy-start.1
  5.5 4.5 %forward.1.x_ref = bf16[4096,256]{1,0:T(8,128)(2,1)S(1)} custom-call(s32[16]{0:T(128)S(1)} %copy-done.3, s32[96]{0:T(128)S(1)} %copy-done.4, s32[96]{0:T(128)S(1)} %copy-done.5, bf16[96,128,128]{2,1,0:T(8,128)(2,1)S(1)} %copy-done, bf16[4096,256]{1,0:T(8,128)(2,1)S(1)} %copy-done.2), custom_call_target="tpu_custom_call" | custom-call | tf_op jit(solution)/shard_map/forward/pallas_call | solution.py:363
  10.0 43.4 %exchange.1 = (bf16[4096,256]{1,0:T(8,128)(2,1)S(1)}, f32[256,256]{1,0:T(8,128)S(1)}) custom-call(bf16[4096,256]{1,0:T(8,128)(2,1)S(1)} %forward.1.x_ref), custom_call_target="tpu_custom_call" | custom-call | tf_op jit(solution)/shard_map/exchange/pallas_call | solution.py:334
  53.4 0.0 copy-done.1
  53.4 65.6 %backward.1 = f32[4096,256]{1,0:T(8,128)} custom-call(s32[16]{0:T(128)S(1)} %copy-done.3, s32[96]{0:T(128)S(1)} %copy-done.4, s32[96]{0:T(128)S(1)} %copy-done.5, bf16[96,128,128]{2,1,0:T(8,128)(2,1)S(1)} %copy-done.1, bf16[4096,256]{1,0:T(8,128)(2,1)S(1)} %get-tuple-element.7.rows_ref, f32[256,256]{1,0:T(8,128)S(1)} %get-tuple-element.8.gram_ref), custom_call_target="tpu_custom_call" | custom-call | tf_op jit(solution)/shard_map/backward/pallas_call | solution.py:378
Async XLA Ops:
  0.0 1.9 %copy-start = (bf16[96,128,128]{2,1,0:T(8,128)(2,1)S(1)}, bf16[96,128,128]{2,1,0:T(8,128)(2,1)}, u32[]{:S(2)}) copy-start(bf16[96,128,128]{2,1,0:T(8,128)(2,1)} %tiles_hbm.3) | copy-start | bytes 9437188
  1.9 1.6 %copy-start.2 = (bf16[4096,256]{1,0:T(8,128)(2,1)S(1)}, bf16[4096,256]{1,0:T(8,128)(2,1)}, u32[]{:S(2)}) copy-start(bf16[4096,256]{1,0:T(8,128)(2,1)} %panel_hbm.1) | copy-start | bytes 6291460
  3.5 0.7 copy-start.3
  4.1 0.7 copy-start.4
  4.8 0.7 copy-start.5
  5.4 48.0 %copy-start.1 = (bf16[96,128,128]{2,1,0:T(8,128)(2,1)S(1)}, bf16[96,128,128]{2,1,0:T(8,128)(2,1)}, u32[]{:S(2)}) copy-start(bf16[96,128,128]{2,1,0:T(8,128)(2,1)} %tiles_hbm.3) | copy-start | bytes 9437188

commit v3 on v2

--- a/solution.py
+++ b/solution.py
@@ -371,7 +371,7 @@
             pltpu.VMEM((height, rank), jnp.float32),
             pltpu.SemaphoreType.DMA((5,)),
         ],
-        compiler_params=params,
+        compiler_params=pltpu.CompilerParams(vmem_limit_bytes=60 * MIB),
         name="forward",
     )(tile_count, tile_doc, tile_col, tile_values, panel)
     rows, gram = exchange(rows, orders_of(n, height))

time: 119 us -> 118 us (level); the launches traced: 119 us -> 117 us
  local copies, waits for them, and re-layouts: 5.45 us -> 1.6 us
    unnamed x12 -> x10, local copies, waits for them, and re-layouts: 5.45 us -> 1.6 us
    pallas_call x1, Pallas kernels: 4.5 us -> 7.83 us  [local(): pl.pallas_call(forward_kernel, out_shape=jax.ShapeDtypeStruct((height, ra...]
    pallas_call x1, Pallas kernels: 43.4 us -> 41.6 us  [exchange(): pl.pallas_call(functools.partial(exchange_kernel, chunks, orders), out_sh...]
where the time goes in v3:
time: 118 us; the launch traced here: 117 us
  Pallas kernels  115 us (97%)
  local copies, waits for them, and re-layouts  1.6 us (1%)
    pallas_call x1, Pallas kernels, local(): pl.pallas_call(backward_kernel, out_shape=jax.ShapeDtypeStruct(panel.shap...  65.6 us
    pallas_call x1, Pallas kernels, exchange(): pl.pallas_call(functools.partial(exchange_kernel, chunks, orders), out_sh...  41.6 us
    pallas_call x1, Pallas kernels, local(): pl.pallas_call(forward_kernel, out_shape=jax.ShapeDtypeStruct((height, ra...  7.83 us

profile of v3, /device:TPU:0, one launch (start us, length us, event | category | flops | bytes accessed | tf_op | source)
XLA Modules:
  0.0 116.7 jit_solution(11043832795947369811)
XLA Ops:
  0.0 0.0 copy-start
  0.0 7.8 %forward.1.x_ref = bf16[4096,256]{1,0:T(8,128)(2,1)} custom-call(s32[16]{0:T(128)} %count_hbm.3, s32[96]{0:T(128)} %doc_hbm.3, s32[96]{0:T(128)} %col_hbm.3, bf16[96,128,128]{2,1,0:T(8,128)(2,1)} %tiles_hbm.3, bf16[4096,256]{1,0:T(8,128)(2,1)} %panel_hbm.1), custom_call_target="tpu_custom_call" | custom-call | tf_op jit(solution)/shard_map/forward/pallas_call | solution.py:363
  7.8 0.0 copy-start.1
  7.8 1.6 %copy-done.1 = bf16[4096,256]{1,0:T(8,128)(2,1)S(1)} copy-done((bf16[4096,256]{1,0:T(8,128)(2,1)S(1)}, bf16[4096,256]{1,0:T(8,128)(2,1)}, u32[]{:S(2)}) %copy-start.1) | copy-done | bytes 2097176
  9.4 0.0 copy-start.2
  9.4 0.0 copy-start.3
  9.4 0.0 copy-start.4
  9.4 41.6 %exchange.1 = (bf16[4096,256]{1,0:T(8,128)(2,1)S(1)}, f32[256,256]{1,0:T(8,128)S(1)}) custom-call(bf16[4096,256]{1,0:T(8,128)(2,1)S(1)} %copy-done.1), custom_call_target="tpu_custom_call" | custom-call | tf_op jit(solution)/shard_map/exchange/pallas_call | solution.py:334
  51.0 0.0 copy-done
  51.0 0.0 copy-done.2
  51.0 0.0 copy-done.3
  51.1 0.0 copy-done.4
  51.1 65.6 %backward.1 = f32[4096,256]{1,0:T(8,128)} custom-call(s32[16]{0:T(128)S(1)} %copy-done.2, s32[96]{0:T(128)S(1)} %copy-done.3, s32[96]{0:T(128)S(1)} %copy-done.4, bf16[96,128,128]{2,1,0:T(8,128)(2,1)S(1)} %copy-done, bf16[4096,256]{1,0:T(8,128)(2,1)S(1)} %get-tuple-element.7.rows_ref, f32[256,256]{1,0:T(8,128)S(1)} %get-tuple-element.8.gram_ref), custom_call_target="tpu_custom_call" | custom-call | tf_op jit(solution)/shard_map/backward/pallas_call | solution.py:378
Async XLA Ops:
  0.0 51.0 %copy-start = (bf16[96,128,128]{2,1,0:T(8,128)(2,1)S(1)}, bf16[96,128,128]{2,1,0:T(8,128)(2,1)}, u32[]{:S(2)}) copy-start(bf16[96,128,128]{2,1,0:T(8,128)(2,1)} %tiles_hbm.3) | copy-start | bytes 9437188
  7.8 1.6 %copy-start.1 = (bf16[4096,256]{1,0:T(8,128)(2,1)S(1)}, bf16[4096,256]{1,0:T(8,128)(2,1)}, u32[]{:S(2)}) copy-start(bf16[4096,256]{1,0:T(8,128)(2,1)} %forward.1.x_ref) | copy-start | bytes 6291460
  9.4 41.6 %copy-start.2 = (s32[16]{0:T(128)S(1)}, s32[16]{0:T(128)}, u32[]{:S(2)}) copy-start(s32[16]{0:T(128)} %count_hbm.3) | copy-start | bytes 196
  9.4 41.6 %copy-start.3 = (s32[96]{0:T(128)S(1)}, s32[96]{0:T(128)}, u32[]{:S(2)}) copy-start(s32[96]{0:T(128)} %doc_hbm.3) | copy-start | bytes 1156
  9.4 41.6 %copy-start.4 = (s32[96]{0:T(128)S(1)}, s32[96]{0:T(128)}, u32[]{:S(2)}) copy-start(s32[96]{0:T(128)} %col_hbm.3) | copy-start | bytes 1156

commit v4 on v3

--- a/solution.py
+++ b/solution.py
@@ -260,7 +260,9 @@
     newton(6, 0.1, dot16)
     error = newton(12, 1e-4, dot32)
 
-    @pl.when(jnp.logical_not(error < 1e-4))
+    turned = jnp.sum(jnp.where(inverse[...] * eye < 0.0, 1.0, 0.0))
+
+    @pl.when(jnp.logical_not(jnp.logical_and(error < 1e-4, turned < 0.5)))
     def _():
         inverse[...] = eye
         lanes = lax.broadcasted_iota(jnp.int32, (1, rank), 1)

time: 118 us -> 118 us (level)
  no operation moved by 1% of the time
where the time goes in v4:
time: 118 us
  Pallas kernels  116 us (98%)
  local copies, waits for them, and re-layouts  1.6 us (1%)
    pallas_call x1, Pallas kernels, local(): pl.pallas_call(backward_kernel, out_shape=jax.ShapeDtypeStruct(panel.shap...  65.8 us
    pallas_call x1, Pallas kernels, exchange(): pl.pallas_call(functools.partial(exchange_kernel, chunks, orders), out_sh...  42.5 us
    pallas_call x1, Pallas kernels, local(): pl.pallas_call(forward_kernel, out_shape=jax.ShapeDtypeStruct((height, ra...  7.83 us

profile of v4, /device:TPU:0, one launch (start us, length us, event | category | flops | bytes accessed | tf_op | source)
XLA Modules:
  0.0 117.8 jit_solution(15069290729643923177)
XLA Ops:
  0.0 0.0 copy-start
  0.0 7.8 %forward.1.x_ref = bf16[4096,256]{1,0:T(8,128)(2,1)} custom-call(s32[16]{0:T(128)} %count_hbm.3, s32[96]{0:T(128)} %doc_hbm.3, s32[96]{0:T(128)} %col_hbm.3, bf16[96,128,128]{2,1,0:T(8,128)(2,1)} %tiles_hbm.3, bf16[4096,256]{1,0:T(8,128)(2,1)} %panel_hbm.1), custom_call_target="tpu_custom_call" | custom-call | tf_op jit(solution)/shard_map/forward/pallas_call | solution.py:365
  7.8 0.0 copy-start.1
  7.8 1.6 %copy-done.1 = bf16[4096,256]{1,0:T(8,128)(2,1)S(1)} copy-done((bf16[4096,256]{1,0:T(8,128)(2,1)S(1)}, bf16[4096,256]{1,0:T(8,128)(2,1)}, u32[]{:S(2)}) %copy-start.1) | copy-done | bytes 2097176
  9.4 0.0 copy-start.2
  9.4 0.0 copy-start.3
  9.4 0.0 copy-start.4
  9.4 42.5 %exchange.1 = (bf16[4096,256]{1,0:T(8,128)(2,1)S(1)}, f32[256,256]{1,0:T(8,128)S(1)}) custom-call(bf16[4096,256]{1,0:T(8,128)(2,1)S(1)} %copy-done.1), custom_call_target="tpu_custom_call" | custom-call | tf_op jit(solution)/shard_map/exchange/pallas_call | solution.py:336
  52.0 0.0 copy-done
  52.0 0.0 copy-done.2
  52.0 0.0 copy-done.3
  52.0 0.0 copy-done.4
  52.0 65.8 %backward.1 = f32[4096,256]{1,0:T(8,128)} custom-call(s32[16]{0:T(128)S(1)} %copy-done.2, s32[96]{0:T(128)S(1)} %copy-done.3, s32[96]{0:T(128)S(1)} %copy-done.4, bf16[96,128,128]{2,1,0:T(8,128)(2,1)S(1)} %copy-done, bf16[4096,256]{1,0:T(8,128)(2,1)S(1)} %get-tuple-element.7.rows_ref, f32[256,256]{1,0:T(8,128)S(1)} %get-tuple-element.8.gram_ref), custom_call_target="tpu_custom_call" | custom-call | tf_op jit(solution)/shard_map/backward/pallas_call | solution.py:380
Async XLA Ops:
  0.0 52.0 %copy-start = (bf16[96,128,128]{2,1,0:T(8,128)(2,1)S(1)}, bf16[96,128,128]{2,1,0:T(8,128)(2,1)}, u32[]{:S(2)}) copy-start(bf16[96,128,128]{2,1,0:T(8,128)(2,1)} %tiles_hbm.3) | copy-start | bytes 9437188
  7.8 1.6 %copy-start.1 = (bf16[4096,256]{1,0:T(8,128)(2,1)S(1)}, bf16[4096,256]{1,0:T(8,128)(2,1)}, u32[]{:S(2)}) copy-start(bf16[4096,256]{1,0:T(8,128)(2,1)} %forward.1.x_ref) | copy-start | bytes 6291460
  9.4 42.5 %copy-start.2 = (s32[16]{0:T(128)S(1)}, s32[16]{0:T(128)}, u32[]{:S(2)}) copy-start(s32[16]{0:T(128)} %count_hbm.3) | copy-start | bytes 196
  9.4 42.5 %copy-start.3 = (s32[96]{0:T(128)S(1)}, s32[96]{0:T(128)}, u32[]{:S(2)}) copy-start(s32[96]{0:T(128)} %doc_hbm.3) | copy-start | bytes 1156
  9.4 42.6 %copy-start.4 = (s32[96]{0:T(128)S(1)}, s32[96]{0:T(128)}, u32[]{:S(2)}) copy-start(s32[96]{0:T(128)} %col_hbm.3) | copy-start | bytes 1156

commit v5 on v4

--- a/solution.py
+++ b/solution.py
@@ -8,7 +8,7 @@
 from jax.sharding import PartitionSpec as P
 
 DOC_BLKS = 32
-GROUP = 8
+GROUP = 12
 MIB = 1024 * 1024
 
 shift_ratio = 0.001

time: 118 us -> 118 us (level); the launches traced: 118 us -> 117 us
  no operation moved by 1% of the time
where the time goes in v5:
time: 118 us; the launch traced here: 117 us
  Pallas kernels  115 us (97%)
  local copies, waits for them, and re-layouts  1.6 us (1%)
    pallas_call x1, Pallas kernels, local(): pl.pallas_call(backward_kernel, out_shape=jax.ShapeDtypeStruct(panel.shap...  65 us
    pallas_call x1, Pallas kernels, exchange(): pl.pallas_call(functools.partial(exchange_kernel, chunks, orders), out_sh...  42.7 us
    pallas_call x1, Pallas kernels, local(): pl.pallas_call(forward_kernel, out_shape=jax.ShapeDtypeStruct((height, ra...  7.18 us

profile of v5, /device:TPU:0, one launch (start us, length us, event | category | flops | bytes accessed | tf_op | source)
XLA Modules:
  0.0 116.6 jit_solution(13934948289470004589)
XLA Ops:
  0.0 0.0 copy-start
  0.0 7.2 %forward.1.x_ref = bf16[4096,256]{1,0:T(8,128)(2,1)} custom-call(s32[16]{0:T(128)} %count_hbm.3, s32[96]{0:T(128)} %doc_hbm.3, s32[96]{0:T(128)} %col_hbm.3, bf16[96,128,128]{2,1,0:T(8,128)(2,1)} %tiles_hbm.3, bf16[4096,256]{1,0:T(8,128)(2,1)} %panel_hbm.1), custom_call_target="tpu_custom_call" | custom-call | tf_op jit(solution)/shard_map/forward/pallas_call | solution.py:365
  7.2 0.0 copy-start.1
  7.2 1.6 %copy-done.1 = bf16[4096,256]{1,0:T(8,128)(2,1)S(1)} copy-done((bf16[4096,256]{1,0:T(8,128)(2,1)S(1)}, bf16[4096,256]{1,0:T(8,128)(2,1)}, u32[]{:S(2)}) %copy-start.1) | copy-done | bytes 2097176
  8.8 0.0 copy-start.2
  8.8 0.0 copy-start.3
  8.8 0.0 copy-start.4
  8.8 42.7 %exchange.1 = (bf16[4096,256]{1,0:T(8,128)(2,1)S(1)}, f32[256,256]{1,0:T(8,128)S(1)}) custom-call(bf16[4096,256]{1,0:T(8,128)(2,1)S(1)} %copy-done.1), custom_call_target="tpu_custom_call" | custom-call | tf_op jit(solution)/shard_map/exchange/pallas_call | solution.py:336
  51.5 0.0 copy-done
  51.5 0.0 copy-done.2
  51.6 0.0 copy-done.3
  51.6 0.0 copy-done.4
  51.6 65.0 %backward.1 = f32[4096,256]{1,0:T(8,128)} custom-call(s32[16]{0:T(128)S(1)} %copy-done.2, s32[96]{0:T(128)S(1)} %copy-done.3, s32[96]{0:T(128)S(1)} %copy-done.4, bf16[96,128,128]{2,1,0:T(8,128)(2,1)S(1)} %copy-done, bf16[4096,256]{1,0:T(8,128)(2,1)S(1)} %get-tuple-element.7.rows_ref, f32[256,256]{1,0:T(8,128)S(1)} %get-tuple-element.8.gram_ref), custom_call_target="tpu_custom_call" | custom-call | tf_op jit(solution)/shard_map/backward/pallas_call | solution.py:380
Async XLA Ops:
  0.0 51.5 %copy-start = (bf16[96,128,128]{2,1,0:T(8,128)(2,1)S(1)}, bf16[96,128,128]{2,1,0:T(8,128)(2,1)}, u32[]{:S(2)}) copy-start(bf16[96,128,128]{2,1,0:T(8,128)(2,1)} %tiles_hbm.3) | copy-start | bytes 9437188
  7.2 1.6 %copy-start.1 = (bf16[4096,256]{1,0:T(8,128)(2,1)S(1)}, bf16[4096,256]{1,0:T(8,128)(2,1)}, u32[]{:S(2)}) copy-start(bf16[4096,256]{1,0:T(8,128)(2,1)} %forward.1.x_ref) | copy-start | bytes 6291460
  8.8 42.8 %copy-start.2 = (s32[16]{0:T(128)S(1)}, s32[16]{0:T(128)}, u32[]{:S(2)}) copy-start(s32[16]{0:T(128)} %count_hbm.3) | copy-start | bytes 196
  8.8 42.8 %copy-start.3 = (s32[96]{0:T(128)S(1)}, s32[96]{0:T(128)}, u32[]{:S(2)}) copy-start(s32[96]{0:T(128)} %doc_hbm.3) | copy-start | bytes 1156
  8.8 42.8 %copy-start.4 = (s32[96]{0:T(128)S(1)}, s32[96]{0:T(128)}, u32[]{:S(2)}) copy-start(s32[96]{0:T(128)} %col_hbm.3) | copy-start | bytes 1156
